TPU v7x, 256 devices: a whole 4x4x8 slice. The times are simulated.
256 devices in a mesh: jobs: 16 (over z, core), tm: 16 (over x, y).
Axes of the slice: x: 4, y: 4, z: 8, core: 2. Of those that a mesh axis runs over, the one named last changes fastest.
Arguments:
- start_density: float32 [16384, 4096], P('jobs', 'tm'), may hold values from 0 to 4
- assign_dual: float32 [16384], P('jobs'), may hold values from -40 to 40
- cap_dual: float32 [2048, 4096], P(None, 'tm'), may hold values from 0 to 2
- tool_of_job: int32 [16384], P('jobs'), may hold values from 0 to 2047
- durations: int32 [16384], P('jobs'), may hold values from 1 to 32, as said below
- releases: int32 [16384], P('jobs'), may hold values from 0 to 4063
- slack: int32 [16384], P('jobs'), may hold values from 0 to 127
- capacity: int32 [2048, 4096], P(None, 'tm'), may hold values from 1 to 7
- job_weight: float32 [16384], P('jobs'), may hold values from 0.5 to 4
- eta: float32 [1], replicated, may hold values from 0.1 to 0.3
- omega: float32 [1], replicated, may hold values from 0.4 to 0.8
Outputs:
- start_out: float32 [16384, 4096], P('jobs', 'tm')
- assign_out: float32 [16384], P('jobs')
- cap_out: float32 [2048, 4096], P('jobs', 'tm')
Inputs may be any that keep to these rules, and one draw needn't show every extreme that they name: `durations`: every job occupies 1 to 32 slots, and some job occupies exactly 32.
All inputs are finite; a program needn't handle non-finite values.
Results may differ from a plain program's by a relative error of at most 0.00011.
Values sent between devices are 32-bit elements; how exact they have to be, the bound alone decides.
A program may use at most 64 MiB of HBM per device.

v0:
```python
import jax
import jax.numpy as jnp
from jax import lax
from jax.sharding import PartitionSpec as P

WIN = 32


def prefix(value, axis, combine, identity):
    peers, position = (lax.axis_size(axis), lax.axis_index(axis))
    everything = lax.all_gather(value, axis)
    start = jnp.broadcast_to(jnp.asarray(identity, value.dtype), value.shape)

    def step(k, before):
        reached = k < position
        new = combine(before, everything[k])
        return jnp.where(reached, new, before)

    return lax.fori_loop(0, peers, step, start)


def passed_along(value, axis, steps):
    count = lax.axis_size(axis)
    first, last = (max(0, -steps), min(count, count - steps))
    return lax.ppermute(value, axis, [(source, source + steps) for source in range(first, last)])


def by_length(source, lengths, forward, block_slots):
    chosen = jnp.zeros((source.shape[0], block_slots), jnp.float32)
    for length in range(1, WIN + 1):
        offset = length if forward else WIN - length
        chosen = jnp.where(lengths == length, source[:, offset : offset + block_slots], chosen)
    return chosen


def shards(
    start_density,
    assign_dual,
    cap_dual,
    tool_of_job,
    durations,
    releases,
    slack,
    capacity,
    job_weight,
    eta,
    omega,
):
    job_rows, block_slots = start_density.shape
    tool_sets = cap_dual.shape[0]
    all_slots = block_slots * lax.axis_size("tm")
    share_rows = tool_sets // lax.axis_size("jobs")
    share_start = lax.axis_index("jobs") * share_rows
    local_slots = jnp.arange(block_slots, dtype=jnp.int32)[None, :]
    slots = local_slots + lax.axis_index("tm") * block_slots
    lengths = durations[:, None]
    span_end = slots + lengths
    allowed = (slots >= releases[:, None]) & (span_end <= all_slots)
    due_slot = releases + durations + slack
    lateness = jnp.maximum(span_end - due_slot[:, None], 0)
    cost = job_weight[:, None] * (
        span_end.astype(jnp.float32) / all_slots + lateness.astype(jnp.float32) / (4 * WIN)
    )
    root = jnp.sqrt(jnp.float32(all_slots))
    weight = omega[0]
    capacity_f = capacity.astype(jnp.float32)
    first_block = lax.axis_index("tm") == 0
    member = (tool_of_job[None, :] == jnp.arange(tool_sets, dtype=jnp.int32)[:, None]).astype(
        jnp.float32
    )

    def share_of(full):
        return lax.dynamic_slice_in_dim(full, share_start, share_rows, 0)

    def rows_of(full):
        return lax.dot_general(
            member,
            full,
            (((0,), (0,)), ((), ())),
            precision=lax.Precision.HIGHEST,
            preferred_element_type=jnp.float32,
        )

    def loads_of(moved):
        partial_cum = jnp.cumsum(moved, axis=1)
        before = prefix(partial_cum[:, -1], "tm", jnp.add, jnp.zeros((job_rows,), jnp.float32))
        cumulative = partial_cum + before[:, None]
        border = passed_along(cumulative[:, block_slots - WIN :], "tm", 1)
        extended = jnp.concatenate([border, cumulative], axis=1)
        earlier = by_length(extended, lengths, False, block_slots)
        window_sums = cumulative - earlier
        return (
            jnp.dot(
                member,
                window_sums,
                precision=lax.Precision.HIGHEST,
                preferred_element_type=jnp.float32,
            )
            / WIN
        )

    def adjoint_of(per_job):
        border = passed_along(per_job[:, :WIN], "tm", -1)
        suffix = lax.cumsum(jnp.concatenate([per_job, border], axis=1), axis=1, reverse=True)
        later = by_length(suffix, lengths, True, block_slots)
        return (suffix[:, :block_slots] - later) / WIN

    def advance(primal, dual_assign, adjoint_now, step_size):
        primal_step = step_size / weight
        dual_step = step_size * weight
        gradient = cost - dual_assign[:, None] / root + adjoint_now
        updated = jnp.where(allowed, jnp.maximum(primal - primal_step * gradient, 0.0), 0.0)
        extrapolated = 2.0 * updated - primal
        partial_loads = loads_of(extrapolated)
        totals_new, totals_old = lax.psum((jnp.sum(updated, axis=1), jnp.sum(primal, axis=1)), "tm")
        assign_next = dual_assign + dual_step * (root - (2.0 * totals_new - totals_old) / root)
        return (updated, assign_next, partial_loads, totals_new - totals_old, dual_step)

    def capacity_duals(partial_loads, dual_state, dual_step, want_rows):
        loads = lax.psum(partial_loads, "jobs")
        full_next = jnp.maximum(dual_state + dual_step * (loads - capacity_f), 0.0)
        per_job = rows_of(full_next) if want_rows else None
        return (full_next, share_of(full_next), per_job)

    share_first = share_of(cap_dual)
    primal = jnp.where(allowed, start_density, 0.0)
    adjoint_first = adjoint_of(rows_of(cap_dual))
    primal_one, assign_one, partial_one, delta_totals, dual_step = advance(
        primal, assign_dual, adjoint_first, eta[0]
    )
    state_one, share_one, rows_one = capacity_duals(partial_one, cap_dual, dual_step, True)
    adjoint_second = adjoint_of(rows_one)
    delta_primal = primal_one - primal
    delta_assign = assign_one - assign_dual
    delta_cap = share_one - share_first
    sum_primal, sum_assign, sum_cap, cross_primal, cross_assign = lax.psum(
        (
            jnp.sum(delta_primal * delta_primal),
            jnp.where(first_block, jnp.sum(delta_assign * delta_assign), 0.0),
            jnp.sum(delta_cap * delta_cap),
            jnp.sum(delta_primal * (adjoint_second - adjoint_first)),
            jnp.where(first_block, jnp.sum(delta_assign * delta_totals), 0.0),
        ),
        ("jobs", "tm"),
    )
    movement = weight / 2.0 * sum_primal + (sum_assign + sum_cap) / (2.0 * weight)
    interaction = jnp.abs(cross_primal - cross_assign / root)
    step_next = movement / (interaction + movement / (1.5 * eta[0]))
    primal_two, assign_two, partial_two, unused_totals, dual_step_two = advance(
        primal_one, assign_one, adjoint_second, step_next
    )
    state_two, share_two, unused_rows = capacity_duals(partial_two, state_one, dual_step_two, False)
    return (primal_two, assign_two, share_two)


def solution(mesh):
    return jax.shard_map(
        shards,
        mesh=mesh,
        in_specs=(
            P("jobs", "tm"),
            P("jobs"),
            P(None, "tm"),
            P("jobs"),
            P("jobs"),
            P("jobs"),
            P("jobs"),
            P(None, "tm"),
            P("jobs"),
            P(),
            P(),
        ),
        out_specs=(P("jobs", "tm"), P("jobs"), P("jobs", "tm")),
        check_vma=False,
    )
```

profile of v0, /device:TPU:8, one launch (start us, length us, event | category | flops | bytes accessed | tf_op | source)
XLA Modules:
  0.0 520.8 jit_solution(9385169852859817230)
XLA Ops:
  7.3 5.9 %fusion.3 = f32[1024,256]{0,1:T(8,128)S(1)} fusion(f32[2048,256]{1,0:T(8,128)} %param.17, s32[1024]{0:T(1024)} %param.18), kind=kOutput, calls=%fused_computation.70 | convolution fusion | flops 6444548096 | bytes 3149824 | tf_op jit(solution)/shard_map/dot_general | solution.py:76
  13.2 4.3 collective-permute-start
  20.6 9.3 %fusion.12 = f32[1024,3,128]{0,1,2:T(4,128)S(1)} fusion(f32[1024,3,128]{0,2,1:T(8,128)S(1)} %bitcast.47), kind=kOutput, calls=%fused_computation.79 | output fusion | flops 49938432 | bytes 3145728 | tf_op jit(solution)/shard_map/reduce-window
  30.5 0.9 copy.20
  31.5 7.5 %multiply_subtract_fusion.1 = (f32[1024,256]{0,1:T(8,128)S(1)}, f32[1024,256]{0,1:T(8,128)S(1)}, f32[1024,256]{0,1:T(8,128)}) fusion(f32[1024,256]{0,1:T(8,128)S(1)} %copy.18, s32[1024]{0:T(1024)S(1)} %copy-done.5, s32[1024]{0:T(1024)S(1)} %copy-done.6, s32[256]{0:T(256)S(1)} %copy-done.15, f32[1024]{0:T(1024)S(1)} %broadcast_multiply_fusion.1, ...), kind=kLoop, calls=%fused_computation.375 | loop fusion | flops 14417920 | bytes 38851588 | tf_op jit(solution)/shard_map/sub | solution.py:113
  40.4 24.3 %all-gather = f32[16384,1]{0,1:T(1,128)S(1)} all-gather(f32[1024,1]{0,1:T(1,128)S(1)} %slice.682), channel_id=2, replica_groups=mesh['jobs'=16,'tm'=16] {'tm'}, dimensions={0}, use_global_device_ids=true | all-gather | bytes 69632 | tf_op jit(solution)/shard_map/all_gather | solution.py:11
  66.9 3.5 collective-permute-start.1
  70.4 3.4 collective-permute-done.1
  73.8 10.2 %fusion.8 = f32[2048,256]{1,0:T(8,128)} fusion(s32[1024]{0:T(1024)S(1)} %copy-done.18, f32[1024,256]{0,1:T(8,128)S(1)} %broadcast_add_fusion.4, f32[1024,32]{0,1:T(8,128)S(1)} %collective-permute-done.1, pred[1024]{0:T(1024)(128)(4,1)S(1)} %copy-done.11, pred[1024]{0:T(1024)(128)(4,1)S(1)} %copy-done.13, pred[1024]{0:T(1024)(128)(4,1)S(1)} %get-tuple-element.232, ...), kind=kOutput, calls=%fused_computation.75 | convolution fusion | flops 6462111744 | bytes 3313664 | tf_op jit(solution)/shard_map/dot_general | solution.py:93
  84.2 117.5 %all-reduce.7.cloned.1.call-done = f32[2048,256]{1,0:T(8,128)} async-done(((f32[2048,256]{1,0:T(8,128)}), f32[2048,256]{1,0:T(8,128)}) %all-reduce.7.cloned.1.call-update) | async-done | bytes 2097168 | tf_op jit(solution)/shard_map/psum | solution.py:120
  201.7 3.3 add_maximum_fusion
  205.0 4.2 fusion.1
  209.2 2.4 collective-permute-start.2
  211.7 1.6 multiply_reduce_fusion.2
  213.3 2.8 collective-permute-done.2
  216.2 9.3 %fusion.10 = f32[1024,3,128]{0,1,2:T(4,128)S(1)} fusion(f32[1024,3,128]{0,2,1:T(8,128)S(1)} %bitcast.48), kind=kOutput, calls=%fused_computation.77 | output fusion | flops 49938432 | bytes 3145728 | tf_op jit(solution)/shard_map/reduce-window.4
  225.5 1.3 copy-done
  226.9 2.1 broadcast_add_fusion
  229.0 0.9 copy.24
  230.2 7.6 %multiply_reduce_fusion = (f32[]{:T(128)}, f32[]{:T(128)}, f32[1024]{0:T(1024)S(1)}, f32[1024]{0:T(1024)S(1)}, f32[1024,256]{0,1:T(8,128)S(1)}) fusion(f32[1024,256]{0,1:T(8,128)S(1)} %copy-done.2, f32[1024,256]{0,1:T(8,128)S(1)} %get-tuple-element.228, f32[1024,256]{0,1:T(8,128)S(1)} %copy.18, s32[1024]{0:T(1024)S(1)} %copy-done.5, s32[1024]{0:T(1024)S(1)} %copy-done.6, ...), kind=kLoop, calls=%fused_computation.373 | loop fusion | flops 12318718 | bytes 38847496 | tf_op jit(solution)/shard_map/reduce_sum | solution.py:141
  237.8 36.8 %all-reduce.3 = (f32[1024]{0:T(1024)S(1)}, f32[1024]{0:T(1024)S(1)}) all-reduce(f32[1024]{0:T(1024)S(1)} %get-tuple-element.198, f32[1024]{0:T(1024)S(1)} %get-tuple-element.199), channel_id=1, replica_groups=mesh['jobs'=16,'tm'=16] {'tm'}, use_global_device_ids=true, to_apply=%region_7.8 | all-reduce | flops 2048 | bytes 16384 | tf_op jit(solution)/shard_map/psum | solution.py:115
  277.1 75.2 %all-reduce.2 = (f32[]{:T(128)}, f32[]{:T(128)}, f32[]{:T(128)}, f32[]{:T(128)}) all-reduce(f32[]{:T(128)} %get-tuple-element.197, f32[]{:T(128)S(6)} %add.173, f32[]{:T(128)} %get-tuple-element.196, f32[]{:T(128)S(6)} %select_n.547), channel_id=1, replica_groups=mesh['jobs'=16,'tm'=16] {'jobs','tm'}, use_global_device_ids=true, to_apply=%region_3.4 | all-reduce | flops 4 | bytes 32 | tf_op jit(solution)/shard_map/psum | solution.py:136
  357.0 21.1 %all-gather.1 = f32[16384,1]{0,1:T(1,128)S(1)} all-gather(f32[1024,1]{0,1:T(1,128)S(1)} %slice.784), channel_id=3, replica_groups=mesh['jobs'=16,'tm'=16] {'tm'}, dimensions={0}, use_global_device_ids=true | all-gather | bytes 69632 | tf_op jit(solution)/shard_map/all_gather | solution.py:11
  379.9 4.4 collective-permute-start.3
  384.3 2.7 collective-permute-done.3
  386.9 10.2 %fusion.9 = f32[2048,256]{1,0:T(8,128)} fusion(s32[1024]{0:T(1024)S(1)} %copy-done.19, f32[1024,256]{0,1:T(8,128)S(1)} %broadcast_add_fusion.2, f32[1024,32]{0,1:T(8,128)S(1)} %collective-permute-done.3, pred[1024]{0:T(1024)(128)(4,1)S(1)} %copy-done.12, pred[1024]{0:T(1024)(128)(4,1)S(1)} %copy-done.14, pred[1024]{0:T(1024)(128)(4,1)S(1)} %get-tuple-element.232, ...), kind=kOutput, calls=%fused_computation.76 | convolution fusion | flops 6462111744 | bytes 3313664 | tf_op jit(solution)/shard_map/dot_general | solution.py:93
  397.2 1.6 copy-done.1
  398.8 1.5 convert_element_type.12
  400.4 1.3 copy.27
  401.7 35.4 %psum.81 = f32[1024]{0:T(1024)S(1)} all-reduce(f32[1024]{0:T(1024)S(1)} %reduce_sum.83), channel_id=1, replica_groups=mesh['jobs'=16,'tm'=16] {'tm'}, use_global_device_ids=true, to_apply=%region_24.25 | all-reduce | flops 1024 | bytes 8192 | tf_op jit(solution)/shard_map/psum | solution.py:115
  437.7 74.1 %all-reduce.9.cloned.1.call-done = f32[2048,256]{1,0:T(8,128)} async-done(((f32[2048,256]{1,0:T(8,128)}), f32[2048,256]{1,0:T(8,128)}) %all-reduce.9.cloned.1.call-update) | async-done | bytes 2097168 | tf_op jit(solution)/shard_map/psum | solution.py:120
  511.8 1.7 fusion.363
  (156 shorter events, 12.4 us)
Async XLA Ops:
  7.2 10.3 %copy-start.5 = (s32[1024]{0:T(1024)S(1)}, s32[1024]{0:T(1024)}, u32[]{:S(2)}) copy-start(s32[1024]{0:T(1024)} %param.19) | copy-start | bytes 12292
  7.2 11.0 %copy-start.6 = (s32[1024]{0:T(1024)S(1)}, s32[1024]{0:T(1024)}, u32[]{:S(2)}) copy-start(s32[1024]{0:T(1024)} %param.20) | copy-start | bytes 12292
  7.2 10.9 %copy-start.17 = (s32[1024]{0:T(1024)S(1)}, s32[1024]{0:T(1024)}, u32[]{:S(2)}) copy-start(s32[1024]{0:T(1024)} %param.21) | copy-start | bytes 12292
  7.2 10.9 %copy-start.7 = (f32[1024]{0:T(1024)S(1)}, f32[1024]{0:T(1024)}, u32[]{:S(2)}) copy-start(f32[1024]{0:T(1024)} %param.16) | copy-start | bytes 12292
  7.2 12.3 %copy-start.4 = (f32[1024,256]{1,0:T(8,128)S(1)}, f32[1024,256]{1,0:T(8,128)}, u32[]{:S(2)}) copy-start(f32[1024,256]{1,0:T(8,128)} %param.15) | copy-start | bytes 3145732
  7.2 194.5 %all-reduce.7.cloned.1.call-start = ((), (), s32[]{:S(2)}) async-start(), calls=%async_computation | async-start | bytes 4194304 | tf_op jit(solution)/shard_map/psum | solution.py:120
  13.2 7.3 %collective-permute-start = (f32[1024,32]{0,1:T(8,128)S(1)}, f32[1024,32]{0,1:T(8,128)S(1)}, u32[]{:S(2)}, u32[]{:S(2)}) collective-permute-start(f32[1024,32]{0,1:T(8,128)S(1)} %slice.644), channel_id=1, source_target_pairs={{1,0},{2,1},{3,2},{4,3},{5,4},{6,5},{7,6},{8,7},{9,8},{10,9},{11,1... | collective-permute-start | bytes 393224 | tf_op jit(solution)/shard_map/ppermute | solution.py:25
  30.5 1.0 copy-start.8
  30.5 1.0 copy-start.9
  30.5 1.0 copy-start.11
  30.5 1.0 copy-start.13
  30.5 1.0 copy-start.15
  40.0 33.8 %copy-start.18 = (s32[1024]{0:T(1024)S(1)}, s32[1024]{0:T(1024)}, u32[]{:S(2)}) copy-start(s32[1024]{0:T(1024)} %param.18) | copy-start | bytes 12292
  66.9 6.9 %collective-permute-start.1 = (f32[1024,32]{0,1:T(8,128)S(1)}, f32[1024,32]{0,1:T(8,128)S(1)}, u32[]{:S(2)}, u32[]{:S(2)}) collective-permute-start(f32[1024,32]{0,1:T(8,128)S(1)} %slice.683), channel_id=1, source_target_pairs={{0,1},{1,2},{2,3},{3,4},{4,5},{5,6},{6,7},{7,8},{8,9},{9,10},{10,1... | collective-permute-start | bytes 393224 | tf_op jit(solution)/shard_map/ppermute | solution.py:25
  84.0 427.8 %all-reduce.9.cloned.1.call-start = ((), (), s32[]{:S(2)}) async-start(), calls=%async_computation.1 | async-start | bytes 4194304 | tf_op jit(solution)/shard_map/psum | solution.py:120
  205.0 4.2 copy-start.3
  209.2 6.9 %collective-permute-start.2 = (f32[1024,32]{0,1:T(8,128)S(1)}, f32[1024,32]{0,1:T(8,128)S(1)}, u32[]{:S(2)}, u32[]{:S(2)}) collective-permute-start(f32[1024,32]{0,1:T(8,128)S(1)} %slice.746), channel_id=1, source_target_pairs={{1,0},{2,1},{3,2},{4,3},{5,4},{6,5},{7,6},{8,7},{9,8},{10,9},{11,1... | collective-permute-start | bytes 393224 | tf_op jit(solution)/shard_map/ppermute | solution.py:25
  225.5 1.3 copy-start
  229.0 1.2 copy-start.2
  229.0 1.2 copy-start.10
  229.0 1.2 copy-start.12
  229.0 1.2 copy-start.14
  229.0 1.2 copy-start.16
  356.7 30.3 %copy-start.19 = (s32[1024]{0:T(1024)S(1)}, s32[1024]{0:T(1024)}, u32[]{:S(2)}) copy-start(s32[1024]{0:T(1024)} %param.18) | copy-start | bytes 12292
  379.9 7.1 %collective-permute-start.3 = (f32[1024,32]{0,1:T(8,128)S(1)}, f32[1024,32]{0,1:T(8,128)S(1)}, u32[]{:S(2)}, u32[]{:S(2)}) collective-permute-start(f32[1024,32]{0,1:T(8,128)S(1)} %slice.785), channel_id=1, source_target_pairs={{0,1},{1,2},{2,3},{3,4},{4,5},{5,6},{6,7},{7,8},{8,9},{9,10},{10,1... | collective-permute-start | bytes 393224 | tf_op jit(solution)/shard_map/ppermute | solution.py:25
  397.2 1.6 copy-start.1
Sparse Core Ops, SparseCore 0:
  84.1 117.5 all-reduce.6
  397.3 114.4 all-reduce.8
where the time goes:
time: 526 us; the launch traced here: 521 us
  waiting for transfers between devices  200 us (38%)
  blocking collectives  193 us (37%)
  other arithmetic  51.8 us (10%)
  matrix products  30.5 us (6%)
  between operations  20.9 us (4%)
  starting transfers between devices  14.9 us (3%)
  local copies, waits for them, and re-layouts  8.36 us (2%)
    psum x2, waiting for transfers between devices, capacity_duals(): loads = lax.psum(partial_loads, 'jobs')  192 us
    psum x1, blocking collectives, shards(): lax.psum((jnp.sum(delta_primal * delta_primal), jnp.where(first_block, jn...  75.2 us
    psum x2, blocking collectives, advance(): lax.psum((jnp.sum(updated, axis=1), jnp.sum(primal, axis=1)), 'tm')  72.2 us
    all_gather x2, blocking collectives, prefix(): everything = lax.all_gather(value, axis)  45.3 us
    another operation x10, other arithmetic  20.6 us
    dot_general x2, matrix products, loads_of(): jnp.dot(member, window_sums, precision=lax.Precision.HIGHEST, preferred_e...  20.4 us
    ppermute x4, starting transfers between devices, passed_along(): lax.ppermute(value, axis, [(source, source + steps) for source in range(f...  14.6 us
  transfers between devices with their start and end apart: 6, of which 5 were waited for; matrix products, arithmetic and copies ran while one was open for 1% of the time, Pallas kernels for 0%

commit v1 on v0

v1 whole, which is shorter than its diff:
```python
import functools
import math
import types

import jax
import jax.numpy as jnp
from jax import lax
from jax.experimental import pallas as pl
from jax.experimental.pallas import tpu as pltpu
from jax.sharding import PartitionSpec as P

WIN = 32
LANES = 128
RING = 8
CORES = 2
F32, BF16 = jnp.float32, jnp.bfloat16
ORDER = (4, 3, 5, 2, 6, 1, 7, 0)
MESSAGES = 7


def window(x, dur, backward):
    n = x.shape[0]

    def move(v, k):
        return pltpu.roll(v, k if backward else n - k, 0)

    d = jnp.broadcast_to(dur, x.shape)
    span, total = 1, x
    acc = jnp.where((d & 1) != 0, x, 0.0)
    while span < WIN // 2:
        total = total + move(total, span)
        span *= 2
        acc = jnp.where((d & span) != 0, total + move(acc, span), acc)
    total = total + move(total, span)
    return jnp.where(d == WIN, total, acc)


def split(x):
    high = x.astype(BF16)
    return high, (x - high.astype(F32)).astype(BF16)


def dot(a, b, contract_b=0):
    return lax.dot_general(
        a, b, (((1,), (contract_b,)), ((), ())), preferred_element_type=F32
    )


def fold(x):
    return jnp.sum(x, axis=0, keepdims=True)


def scratch_of(rows, slots, tools, share, blocks, ny, nx):
    half = slots // 2
    dma, vmem = pltpu.SemaphoreType.DMA, pltpu.VMEM
    return dict(
        sd_v=vmem((rows, slots), F32),
        cap_v=vmem((tools, slots), F32),
        capac_v=vmem((share, slots), jnp.int32),
        cap_hi=vmem((tools, slots), BF16),
        cap_lo=vmem((tools, slots), BF16),
        mem=vmem((rows, tools), BF16),
        pj0=vmem((slots, rows), F32),
        pj1=vmem((slots, rows), F32),
        p0=vmem((slots, rows), F32),
        p1=vmem((slots, rows), F32),
        ex=vmem((slots, rows), F32),
        wdp=vmem((slots, rows), F32),
        grad=vmem((slots, rows), F32),
        ws=vmem((2 * slots, rows), BF16),
        hpj=vmem((2, WIN, rows), F32),
        hp=vmem((3, WIN, rows), F32),
        part=vmem((RING, CORES, slots, share), F32),
        pairbuf=vmem((2, RING, slots, share), F32),
        rsu=vmem((2, MESSAGES, half, share), F32),
        rsd=vmem((2, MESSAGES, half, share), F32),
        ag=vmem((RING, CORES, slots, share), F32),
        cap_s=vmem((slots, share), F32),
        capac_s=vmem((slots, share), F32),
        yrow=vmem((ny, 2 * blocks, LANES), F32),
        xrow=vmem((nx, 2 * blocks, LANES), F32),
        yrow2=vmem((ny, blocks, LANES), F32),
        xrow2=vmem((nx, blocks, LANES), F32),
        tot1=vmem((blocks, LANES), F32),
        a1=vmem((blocks, LANES), F32),
        accp=vmem((8, LANES), F32),
        sc_c=vmem((CORES, 8, LANES), F32),
        sc_z=vmem((RING, 8, LANES), F32),
        sc_y=vmem((ny, 8, LANES), F32),
        sc_x=vmem((nx, 8, LANES), F32),
        s_load=dma((3,)),
        s_out=dma((1,)),
        s_halo=dma((2, 5)),
        s_up=dma((2, 3, MESSAGES)),
        s_dn=dma((2, 3, MESSAGES)),
        s_pair=dma((2, 2, RING)),
        s_sib=dma((2, 2 * RING)),
        s_rowy=dma((2, 2, ny)),
        s_rowx=dma((2, 2, nx)),
        s_scc=dma((2, CORES)),
        s_scz=dma((2, RING)),
        s_scy=dma((2, ny)),
        s_scx=dma((2, nx)),
    )


def kernel(
    names, ny, nx, all_slots, sd, cap, capac, tool, dur, rel, slack, jw, assign, eta, omega,
    out_p, out_a, out_c, *scratch,
):
    r = types.SimpleNamespace(**dict(zip(names, scratch)))
    rows, slots = r.sd_v.shape
    tools, share = r.cap_v.shape[0], r.capac_v.shape[0]
    blocks, half, ntm = rows // LANES, slots // 2, ny * nx
    pair = CORES * share
    root = math.sqrt(all_slots)

    mj, mt = lax.axis_index("jobs"), lax.axis_index("tm")
    z, c = lax.div(mj, CORES), lax.rem(mj, CORES)
    x, y = lax.div(mt, ny), lax.rem(mt, ny)

    def zline(k):
        return lax.rem(z + k, RING) * CORES + c

    sibling = (z * CORES + 1 - c, mt)
    above, below = (zline(1), mt), (zline(RING - 1), mt)
    after, before = (mj, lax.rem(mt + 1, ntm)), (mj, lax.rem(mt + ntm - 1, ntm))
    z_peers = [(lax.rem(z + k, RING), (zline(k), mt)) for k in range(1, RING)]
    y_peers = [(lax.rem(y + k, ny), (mj, x * ny + lax.rem(y + k, ny))) for k in range(1, ny)]
    x_peers = [(lax.rem(x + k, nx), (mj, lax.rem(x + k, nx) * ny + y)) for k in range(1, nx)]

    sent = []

    def remote(src, dst, ssem, rsem, device):
        return pltpu.make_async_remote_copy(
            src_ref=src, dst_ref=dst, send_sem=ssem, recv_sem=rsem,
            device_id=device, device_id_type=pl.DeviceIdType.MESH,
        )

    def send(*args):
        copy = remote(*args)
        copy.start()
        sent.append(copy)

    def arrived(dst, ssem, rsem, device):
        remote(dst, dst, ssem, rsem, device).wait_recv()

    def drain():
        for copy in sent:
            copy.wait_send()
        sent.clear()

    def spread(buf, mine, peers, ssem, rsem):
        for k, (_, device) in enumerate(peers):
            send(buf.at[mine], buf.at[mine], ssem.at[k], rsem.at[mine], device)

        def wait():
            for k, (index, device) in enumerate(peers):
                arrived(buf.at[index], ssem.at[k], rsem.at[index], device)

        return wait

    def added(buf):
        total = buf[0]
        for k in range(1, buf.shape[0]):
            total = total + buf[k]
        return total

    first_tool = pl.multiple_of(mj * share, share)
    loads = [
        pltpu.make_async_copy(cap, r.cap_v, r.s_load.at[0]),
        pltpu.make_async_copy(sd, r.sd_v, r.s_load.at[1]),
        pltpu.make_async_copy(capac.at[pl.ds(first_tool, share), :], r.capac_v, r.s_load.at[2]),
    ]
    for copy in loads:
        copy.start()
    barrier = pltpu.get_barrier_semaphore()
    partners = [sibling, after, before]
    partners += [device for group in (z_peers, y_peers, x_peers) for _, device in group]
    for device in partners:
        pl.semaphore_signal(barrier, inc=1, device_id=device, device_id_type=pl.DeviceIdType.MESH)

    weight = omega[0]
    tau1, sigma1 = eta[0] / weight, eta[0] * weight

    lane = lax.broadcasted_iota(jnp.int32, (LANES, LANES), 1).astype(F32)

    @pl.loop(0, blocks)
    def _(b):
        row = jnp.broadcast_to(tool[pl.ds(b, 1), :].astype(F32), (LANES, LANES))
        column = row.T
        for k in range(tools // LANES):
            hit = jnp.where(column == lane + float(k * LANES), 1.0, 0.0).astype(BF16)
            r.mem[pl.ds(pl.multiple_of(b * LANES, LANES), LANES), k * LANES : (k + 1) * LANES] = hit

    loads[0].wait()

    @pl.loop(0, tools // share)
    def _(b):
        at = pl.ds(pl.multiple_of(b * share, share), share)
        high, low = split(r.cap_v[at, :])
        r.cap_hi[at, :] = high
        r.cap_lo[at, :] = low

    step = min(rows, 256)

    @pl.loop(0, rows // step)
    def _(b):
        at = pl.ds(pl.multiple_of(b * step, step), step)
        m = r.mem[at, :]
        found = dot(m, r.cap_hi[...]) + dot(m, r.cap_lo[...])
        r.pj0[:, at] = found.T

    def lanes_of(b):
        return pl.ds(pl.multiple_of(b * LANES, LANES), LANES)

    first_slot = mt * slots
    slot = lax.broadcasted_iota(jnp.int32, (slots, LANES), 0) + first_slot

    def allowed_of(b):
        return (slot >= rel[pl.ds(b, 1), :]) & (slot + dur[pl.ds(b, 1), :] <= all_slots)

    def cost_of(b):
        d = dur[pl.ds(b, 1), :]
        due = rel[pl.ds(b, 1), :] + d + slack[pl.ds(b, 1), :]
        end = slot + d
        late = jnp.maximum(end - due, 0)
        return jw[pl.ds(b, 1), :] * (
            end.astype(F32) * (1.0 / all_slots) + late.astype(F32) * (1.0 / (4 * WIN))
        )

    pl.semaphore_wait(barrier, len(partners))

    def halo(k, src, dst, device):
        send(src, dst, r.s_halo.at[0, k], r.s_halo.at[1, k], device)

    def halo_arrived(k, dst, device):
        arrived(dst, r.s_halo.at[0, k], r.s_halo.at[1, k], device)

    head, tail = pl.ds(0, WIN), pl.ds(slots - WIN, WIN)
    halo(0, r.pj0.at[head, :], r.hpj.at[0], before)

    loads[1].wait()

    @pl.loop(0, blocks)
    def _(b):
        start = r.sd_v[lanes_of(b), :].T
        p = jnp.where(allowed_of(b), start, 0.0)
        r.p0[:, lanes_of(b)] = p
        r.yrow[y, pl.ds(blocks + b, 1), :] = fold(p)

    halo(1, r.p0.at[tail, :], r.hp.at[0], after)

    loads[2].wait()
    r.cap_s[...] = r.cap_v[pl.ds(first_tool, share), :].T
    r.capac_s[...] = r.capac_v[...].astype(F32).T

    def extended(k, buf, b):
        below_rows = jnp.where(mt == ntm - 1, 0.0, r.hpj[k, :, lanes_of(b)])
        return jnp.concatenate([buf[:, lanes_of(b)], below_rows], axis=0)

    def preceded(k, buf, b):
        above_rows = jnp.where(mt == 0, 0.0, r.hp[k, :, lanes_of(b)])
        return jnp.concatenate([above_rows, buf[:, lanes_of(b)]], axis=0)

    halo_arrived(0, r.hpj.at[0], after)
    r.accp[...] = jnp.zeros_like(r.accp)

    @pl.loop(0, blocks)
    def _(b):
        d = dur[pl.ds(b, 1), :]
        adj = window(extended(0, r.pj0, b), d, False)[:slots] * (1.0 / WIN)
        p = r.p0[:, lanes_of(b)]
        gradient = cost_of(b) - assign[pl.ds(b, 1), :] * (1.0 / root) + adj
        new = jnp.where(allowed_of(b), jnp.maximum(p - tau1 * gradient, 0.0), 0.0)
        r.p1[:, lanes_of(b)] = new
        r.ex[:, lanes_of(b)] = 2.0 * new - p
        r.yrow[y, pl.ds(b, 1), :] = fold(new)
        moved = new - p
        r.accp[0:1, :] += fold(moved * moved)

    halo(2, r.ex.at[tail, :], r.hp.at[1], after)
    rows_y = spread(r.yrow, y, y_peers, r.s_rowy.at[0, 0], r.s_rowy.at[0, 1])

    halo_arrived(1, r.hp.at[0], before)

    @pl.loop(0, blocks)
    def _(b):
        d = dur[pl.ds(b, 1), :]
        r.wdp[:, lanes_of(b)] = window(preceded(0, r.p0, b), d, True)[WIN:]

    halo_arrived(2, r.hp.at[1], before)

    @pl.loop(0, blocks)
    def _(b):
        d = dur[pl.ds(b, 1), :]
        w = window(preceded(1, r.ex, b), d, True)[WIN:]
        r.wdp[:, lanes_of(b)] = 0.5 * (w - r.wdp[:, lanes_of(b)])
        high, low = split(w)
        r.ws[0:slots, lanes_of(b)] = high
        r.ws[slots : 2 * slots, lanes_of(b)] = low

    def reduced_loads(it, extra):
        paired = set()

        def produce(i):
            owner = lax.rem(z + ORDER[i], RING)
            full = dot(r.ws[...], r.mem[:, pl.ds(pl.multiple_of(owner * pair, pair), pair)])
            full = (full[:slots] + full[slots:]) * (1.0 / WIN)
            r.part[i, 0] = full[:, :share]
            r.part[i, 1] = full[:, share:]
            send(r.part.at[i, 1 - c], r.pairbuf.at[it, i], r.s_pair.at[it, 0, i], r.s_pair.at[it, 1, i], sibling)

        def mine(i, side):
            if i not in paired:
                arrived(r.pairbuf.at[it, i], r.s_pair.at[it, 0, i], r.s_pair.at[it, 1, i], sibling)
                paired.add(i)
            at = pl.ds(side * half, half)
            return r.part[i, c, at, :] + r.pairbuf[it, i, at, :]

        def message(m, upward):
            buf, sems = (r.rsu, r.s_up) if upward else (r.rsd, r.s_dn)
            to, source = (above, below) if upward else (below, above)
            distance = 4 - (m + 1) // 2
            i = ORDER.index(distance if upward else RING - distance)
            side = m % 2 if upward else 1 - m % 2
            value = mine(i, side)
            if m >= 2:
                arrived(buf.at[it, m - 2], sems.at[it, 0, m - 2], sems.at[it, 1, m - 2], source)
                value = value + buf[it, m - 2]
            at = pl.ds(side * half, half)
            r.part[i, c, at, :] = value
            send(r.part.at[i, c, at, :], buf.at[it, m], sems.at[it, 0, m], sems.at[it, 1, m], to)

        ready = {0: 3, 1: 5, 2: 7, 3: 8}
        done = 0
        for m in range(MESSAGES):
            while done < ready.get(m, RING):
                produce(done)
                done += 1
            message(m, True)
            message(m, False)
            extra(m)
        out = []
        own = ORDER.index(0)
        for side in (0, 1):
            value = mine(own, side)
            for upward, buf, sems, source in ((True, r.rsu, r.s_up, below), (False, r.rsd, r.s_dn, above)):
                m = 6 - side if upward else 5 + side
                arrived(buf.at[it, m], sems.at[it, 0, m], sems.at[it, 1, m], source)
                value = value + buf[it, m]
            out.append(value)
        return jnp.concatenate(out, axis=0)

    def rows_first(m):
        if m == 1:
            rows_y()
            r.xrow[x] = added(r.yrow)
            rows_first.wait = spread(r.xrow, x, x_peers, r.s_rowx.at[0, 0], r.s_rowx.at[0, 1])
        if m == 4:
            rows_first.wait()
            total = added(r.xrow)
            new, old = total[:blocks], total[blocks:]
            r.tot1[...] = new
            delta = sigma1 * (root - (2.0 * new - old) * (1.0 / root))
            r.a1[...] = assign[...] + delta
            lead = jnp.where(mt == 0, 1.0, 0.0)
            r.accp[3:4, :] = lead * fold(delta * delta)
            r.accp[4:5, :] = lead * fold(delta * (new - old))

    loads1 = reduced_loads(0, rows_first)
    cap1 = jnp.maximum(r.cap_s[...] + sigma1 * (loads1 - r.capac_s[...]), 0.0)
    delta_cap = cap1 - r.cap_s[...]
    r.accp[1:2, :] = fold(delta_cap * delta_cap)
    r.ag[z, c] = cap1
    drain()

    def part_of(hops, side):
        return (lax.rem(z + hops + RING, RING), c, pl.ds(side * half, half), slice(None))

    def pass_on(m, upward):
        sems, to = (r.s_up, above) if upward else (r.s_dn, below)
        hops = -(m // 2) if upward else m // 2
        at = part_of(hops, m % 2 if upward else 1 - m % 2)
        send(r.ag.at[at], r.ag.at[at], sems.at[0, 2, m], sems.at[1, 2, m], to)

    def across(hops, side):
        k = 2 * (hops % RING) + side
        at = part_of(hops, side)
        send(r.ag.at[at], r.ag.at[at], r.s_sib.at[0, k], r.s_sib.at[1, k], sibling)

    def crossed(hops, side):
        k = 2 * (hops % RING) + side
        at = (lax.rem(z + hops + RING, RING), 1 - c, pl.ds(side * half, half), slice(None))
        arrived(r.ag.at[at], r.s_sib.at[0, k], r.s_sib.at[1, k], sibling)

    def gather(hops, first=False):
        crossed(hops, 0)
        crossed(hops, 1)
        owner = lax.rem(z + hops + RING, RING)
        high, low = split(jnp.concatenate([r.ag[owner, 0], r.ag[owner, 1]], axis=1))
        both = jnp.concatenate([high, low], axis=0)
        full = dot(both, r.mem[:, pl.ds(pl.multiple_of(owner * pair, pair), pair)], 1)
        full = full[:slots] + full[slots:]
        r.pj1[...] = full if first else r.pj1[...] + full

    for m in (0, 1):
        pass_on(m, True)
        pass_on(m, False)
    across(0, 0)
    across(0, 1)
    work = {0: (0,), 2: (-1,), 3: (1,), 4: (-2,), 5: (2,), 6: (-3, 3)}
    for m in range(MESSAGES):
        for upward in (True, False):
            hops = -1 - m // 2 if upward else 1 + m // 2
            side = m % 2 if upward else 1 - m % 2
            sems, source = (r.s_up, below) if upward else (r.s_dn, above)
            arrived(r.ag.at[part_of(hops, side)], sems.at[0, 2, m], sems.at[1, 2, m], source)
            if m + 2 < MESSAGES:
                pass_on(m + 2, upward)
            across(hops, side)
        for hops in work.get(m, ()):
            gather(hops, first=hops == 0)
    gather(4)

    halo(3, r.pj1.at[head, :], r.hpj.at[1], before)

    @pl.loop(0, blocks)
    def _(b):
        at = lanes_of(b)
        r.accp[2:3, :] += fold((r.pj1[:, at] - r.pj0[:, at]) * r.wdp[:, at]) * (1.0 / WIN)

    r.sc_c[c] = r.accp[...]
    wait = spread(r.sc_c, c, [(1 - c, sibling)], r.s_scc.at[0], r.s_scc.at[1])
    wait()
    r.sc_z[z] = added(r.sc_c)
    wait = spread(r.sc_z, z, z_peers, r.s_scz.at[0], r.s_scz.at[1])
    halo_arrived(3, r.hpj.at[1], after)

    def second_gradient(b):
        d = dur[pl.ds(b, 1), :]
        adj = window(extended(1, r.pj1, b), d, False)[:slots] * (1.0 / WIN)
        r.grad[:, lanes_of(b)] = cost_of(b) - r.a1[pl.ds(b, 1), :] * (1.0 / root) + adj

    third = max(blocks // 3, 1)
    pl.loop(0, third)(second_gradient)
    wait()
    r.sc_y[y] = added(r.sc_z)
    wait = spread(r.sc_y, y, y_peers, r.s_scy.at[0], r.s_scy.at[1])
    pl.loop(third, 2 * third)(second_gradient)
    wait()
    r.sc_x[x] = added(r.sc_y)
    wait = spread(r.sc_x, x, x_peers, r.s_scx.at[0], r.s_scx.at[1])
    if blocks > 2 * third:
        pl.loop(2 * third, blocks)(second_gradient)
    wait()
    sums = jnp.sum(added(r.sc_x), axis=1, keepdims=True)
    sum_primal, sum_cap, cross_primal, sum_assign, cross_assign = (sums[k : k + 1] for k in range(5))
    movement = weight * 0.5 * sum_primal + (sum_assign + sum_cap) / (2.0 * weight)
    interaction = jnp.abs(cross_primal - cross_assign * (1.0 / root))
    step_next = movement / (interaction + movement / (1.5 * eta[0]))
    tau2 = jnp.broadcast_to(step_next / weight, (1, LANES))
    sigma2 = jnp.broadcast_to(step_next * weight, (1, LANES))

    @pl.loop(0, blocks)
    def _(b):
        at = lanes_of(b)
        p = r.p1[:, at]
        new = jnp.where(allowed_of(b), jnp.maximum(p - tau2 * r.grad[:, at], 0.0), 0.0)
        r.p0[:, at] = new
        r.ex[:, at] = 2.0 * new - p
        r.yrow2[y, pl.ds(b, 1), :] = fold(new)

    drain()
    halo(4, r.ex.at[tail, :], r.hp.at[2], after)
    rows2_y = spread(r.yrow2, y, y_peers, r.s_rowy.at[1, 0], r.s_rowy.at[1, 1])

    @pl.loop(0, blocks)
    def _(b):
        r.sd_v[lanes_of(b), :] = r.p0[:, lanes_of(b)].T

    store = pltpu.make_async_copy(r.sd_v, out_p, r.s_out.at[0])
    store.start()
    halo_arrived(4, r.hp.at[2], before)

    @pl.loop(0, blocks)
    def _(b):
        d = dur[pl.ds(b, 1), :]
        high, low = split(window(preceded(2, r.ex, b), d, True)[WIN:])
        r.ws[0:slots, lanes_of(b)] = high
        r.ws[slots : 2 * slots, lanes_of(b)] = low

    def rows_second(m):
        if m == 1:
            rows2_y()
            r.xrow2[x] = added(r.yrow2)
            rows_second.wait = spread(r.xrow2, x, x_peers, r.s_rowx.at[1, 0], r.s_rowx.at[1, 1])
        if m == 4:
            rows_second.wait()
            new = added(r.xrow2)
            out_a[...] = r.a1[...] + sigma2 * (root - (2.0 * new - r.tot1[...]) * (1.0 / root))

    loads2 = reduced_loads(1, rows_second)
    cap2 = jnp.maximum(r.ag[z, c] + sigma2 * (loads2 - r.capac_s[...]), 0.0)
    out_c[...] = cap2.T
    drain()
    store.wait()


def shards(sizes, all_slots, start, assign, cap, tool, dur, rel, slack, capac, jw, eta, omega):
    ny, nx = sizes
    rows, slots = start.shape
    tools = cap.shape[0]
    share = tools // (RING * CORES)
    blocks = rows // LANES
    scratch = scratch_of(rows, slots, tools, share, blocks, ny, nx)
    hbm = pl.BlockSpec(memory_space=pl.ANY)
    vec = pl.BlockSpec(memory_space=pltpu.VMEM)
    smem = pl.BlockSpec(memory_space=pltpu.SMEM)

    def tiles(v):
        return v.reshape(blocks, LANES)

    p, a, c = pl.pallas_call(
        functools.partial(kernel, tuple(scratch), ny, nx, all_slots),
        out_shape=(
            jax.ShapeDtypeStruct((rows, slots), F32),
            jax.ShapeDtypeStruct((blocks, LANES), F32),
            jax.ShapeDtypeStruct((share, slots), F32),
        ),
        in_specs=[hbm, hbm, hbm] + [vec] * 6 + [smem] * 2,
        out_specs=(hbm, vec, vec),
        scratch_shapes=list(scratch.values()),
        compiler_params=pltpu.CompilerParams(
            collective_id=0, has_side_effects=True, vmem_limit_bytes=56 * 1024 * 1024
        ),
        cost_estimate=pl.CostEstimate(flops=8_600_000_000, bytes_accessed=6_000_000, transcendentals=0),
        name="pdhg",
    )(start, cap, capac, *map(tiles, (tool, dur, rel, slack, jw, assign)), eta, omega)
    return p, a.reshape(rows), c


def solution(mesh):
    ntm = mesh.shape["tm"]
    ny = 4 if ntm >= 16 else ntm

    def run(start, *rest):
        body = functools.partial(shards, (ny, ntm // ny), start.shape[1])
        return jax.shard_map(
            body,
            mesh=mesh,
            in_specs=(
                P("jobs", "tm"), P("jobs"), P(None, "tm"), P("jobs"), P("jobs"), P("jobs"),
                P("jobs"), P(None, "tm"), P("jobs"), P(), P(),
            ),
            out_specs=(P("jobs", "tm"), P("jobs"), P("jobs", "tm")),
            check_vma=False,
        )(start, *rest)

    return run
```

time: 526 us -> 104 us (0.20)
  waiting for transfers between devices: 200 us -> 0 us
  blocking collectives: 193 us -> 0 us
  Pallas kernels: 0 us -> 97.9 us
  other arithmetic: 51.8 us -> 0 us
  matrix products: 30.5 us -> 0 us
  between operations: 20.9 us -> 1.95 us
  starting transfers between devices: 14.9 us -> 0 us
    psum x2 -> x0, waiting for transfers between devices: 192 us -> none  [capacity_duals(): loads = lax.psum(partial_loads, 'jobs')]
    psum x3 -> x0, blocking collectives: 147 us -> none  [the longest x1 75.2 us: shards(): lax.psum((jnp.sum(delta_primal * delta_primal), jnp.where(first_block, jn...]
    pallas_call x0 -> x1, Pallas kernels: none -> 97.9 us  [shards(): pl.pallas_call(functools.partial(kernel, tuple(scratch), ny, nx, all_slot...]
    all_gather x2 -> x0, blocking collectives: 45.3 us -> none  [prefix(): everything = lax.all_gather(value, axis)]
    dot_general x4 -> x0, matrix products: 30.5 us -> none  [the longest x2 20.4 us: loads_of(): jnp.dot(member, window_sums, precision=lax.Precision.HIGHEST, preferred_e...]
    another operation x12 -> x0, other arithmetic: 23.1 us -> none
    ppermute x4 -> x0, starting transfers between devices: 14.6 us -> none  [passed_along(): lax.ppermute(value, axis, [(source, source + steps) for source in range(f...]
    reduce_sum x4 -> x0, other arithmetic: 9.87 us -> none  [the longest x1 7.57 us: shards(): jnp.sum(delta_primal * (adjoint_second - adjoint_first))]
  transfers between devices with their start and end apart: 6 -> 0, of which waited for: 5 -> 0; matrix products, arithmetic and copies ran while one was open for 1% -> 0% of each run, Pallas kernels for 0% -> 0%
where the time goes in v1:
time: 104 us; the launch traced here: 103 us
  Pallas kernels  97.9 us (94%)
  local copies, waits for them, and re-layouts  3.55 us (3%)
  between operations  1.95 us (2%)
    pallas_call x1, Pallas kernels, shards(): pl.pallas_call(functools.partial(kernel, tuple(scratch), ny, nx, all_slot...  97.9 us
    unnamed x7, local copies, waits for them, and re-layouts  3.55 us

profile of v1, /device:TPU:8, one launch (start us, length us, event | category | flops | bytes accessed | tf_op | source)
XLA Modules:
  0.0 103.4 jit_solution(16223071710495683565)
XLA Ops:
  1.9 97.9 %pdhg.1 = (f32[1024,256]{1,0:T(8,128)}, f32[8,128]{1,0:T(8,128)}, f32[128,256]{1,0:T(8,128)}) custom-call(f32[1024,256]{1,0:T(8,128)} %sd.1, f32[2048,256]{1,0:T(8,128)} %cap.1, s32[2048,256]{1,0:T(8,128)} %capac.1, s32[8,128]{1,0:T(8,128)} %bitcast.8, s32[8,128]{1,0:T(8,128)} %bitcast.9, s32[8,128]{1,0:T(8,128)} %bitcast.10, s32[8,128]{1,0:T(8,128)} %bitcast.11, ...), custom_call_target="tpu_custom_call" | custom-call | flops 8600000512 | bytes 6000000 | tf_op jit(solution)/shard_map/pdhg/pallas_call | solution.py:524
  99.8 0.0 copy-start.1
  99.8 0.0 copy-start
  99.8 2.3 %copy.19 = f32[1024,256]{1,0:T(8,128)} copy(f32[1024,256]{1,0:T(8,128)} %get-tuple-element.12) | data formatting | bytes 2097152
  102.1 0.0 copy-done.1
  102.1 0.6 copy.20
  102.7 0.0 copy-done
  102.7 0.7 copy.21
Async XLA Ops:
  99.8 2.3 %copy-start.1 = (f32[8,128]{1,0:T(8,128)S(1)}, f32[8,128]{1,0:T(8,128)}, u32[]{:S(2)}) copy-start(f32[8,128]{1,0:T(8,128)} %get-tuple-element.7) | copy-start | bytes 12292
  99.8 2.9 %copy-start = (f32[128,256]{1,0:T(8,128)S(1)}, f32[128,256]{1,0:T(8,128)}, u32[]{:S(2)}) copy-start(f32[128,256]{1,0:T(8,128)} %get-tuple-element.14) | copy-start | bytes 393220

commit v2 on v1

v2 whole, which is shorter than its diff:
```python
import functools
import math
import types

import jax
import jax.numpy as jnp
from jax import lax
from jax.experimental import pallas as pl
from jax.experimental.pallas import tpu as pltpu
from jax.sharding import PartitionSpec as P

WIN = 32
LANES = 128
RING = 8
CORES = 2
F32, BF16 = jnp.float32, jnp.bfloat16
ORDER = (4, 3, 5, 2, 6, 1, 7, 0)
MESSAGES = 7
PIECES = 2


def window(x, dur, backward):
    n = x.shape[0]

    def move(v, k):
        return pltpu.roll(v, k if backward else n - k, 0)

    d = jnp.broadcast_to(dur, x.shape)
    span, total = 1, x
    acc = jnp.where((d & 1) != 0, x, 0.0)
    while span < WIN // 2:
        total = total + move(total, span)
        span *= 2
        acc = jnp.where((d & span) != 0, total + move(acc, span), acc)
    total = total + move(total, span)
    return jnp.where(d == WIN, total, acc)


def split(x):
    high = x.astype(BF16)
    return high, (x - high.astype(F32)).astype(BF16)


def dot(a, b, contract_b=0):
    return lax.dot_general(
        a, b, (((1,), (contract_b,)), ((), ())), preferred_element_type=F32
    )


def fold(x):
    return jnp.sum(x, axis=0, keepdims=True)


def scratch_of(rows, slots, tools, share, blocks, ny, nx):
    piece = slots // (2 * PIECES)
    dma, vmem = pltpu.SemaphoreType.DMA, pltpu.VMEM
    return dict(
        ints=vmem((4, blocks, LANES), jnp.int32),
        floats=vmem((2, blocks, LANES), F32),
        eta=pltpu.SMEM((1,), F32),
        omega=pltpu.SMEM((1,), F32),
        sd_v=vmem((rows, slots), F32),
        cap_v=vmem((tools, slots), F32),
        capac_v=vmem((share, slots), jnp.int32),
        cap_hi=vmem((tools, slots), BF16),
        cap_lo=vmem((tools, slots), BF16),
        mem=vmem((rows, tools), BF16),
        pj0=vmem((slots + 2 * WIN, rows), F32),
        pj1=vmem((slots + 2 * WIN, rows), F32),
        p0=vmem((slots + WIN, rows), F32),
        p1=vmem((slots + WIN, rows), F32),
        grad=vmem((slots + WIN, rows), F32),
        wdp=vmem((slots, rows), F32),
        ws=vmem((2 * slots, rows), BF16),
        part=vmem((RING, CORES, slots, share), F32),
        pairbuf=vmem((2, RING, slots, share), F32),
        rsu=vmem((2, MESSAGES, PIECES, piece, share), F32),
        rsd=vmem((2, MESSAGES, PIECES, piece, share), F32),
        ag=vmem((RING, CORES, slots, share), F32),
        cap_s=vmem((slots, share), F32),
        capac_s=vmem((slots, share), F32),
        c2=vmem((slots, share), F32),
        yrow=vmem((ny, 2 * blocks, LANES), F32),
        xrow=vmem((nx, 2 * blocks, LANES), F32),
        yrow2=vmem((ny, blocks, LANES), F32),
        xrow2=vmem((nx, blocks, LANES), F32),
        tot1=vmem((blocks, LANES), F32),
        a1=vmem((blocks, LANES), F32),
        accp=vmem((8, LANES), F32),
        sc_c=vmem((CORES, 8, LANES), F32),
        sc_z=vmem((RING, 8, LANES), F32),
        sc_t=vmem((ny * nx, 8, LANES), F32),
        s_load=dma((11,)),
        s_out=dma((1,)),
        s_halo=dma((2, 5)),
        s_up=dma((2, 3, MESSAGES, PIECES)),
        s_dn=dma((2, 3, MESSAGES, PIECES)),
        s_pair=dma((2, 2, RING)),
        s_sib=dma((2, 2 * RING)),
        s_rowy=dma((2, 2, ny)),
        s_rowx=dma((2, 2, nx)),
        s_scc=dma((2, CORES)),
        s_scz=dma((2, RING)),
        s_sct=dma((2, ny * nx)),
    )


def kernel(
    names, ny, nx, all_slots, sd, cap, capac, tool_in, dur_in, rel_in, slack_in, jw_in, assign_in,
    eta_in, omega_in, out_p, out_a, out_c, *scratch,
):
    r = types.SimpleNamespace(**dict(zip(names, scratch)))
    rows, slots = r.sd_v.shape
    tools, share = r.cap_v.shape[0], r.capac_v.shape[0]
    blocks, half, ntm = rows // LANES, slots // 2, ny * nx
    piece = half // PIECES
    pair = CORES * share
    root = math.sqrt(all_slots)

    mj, mt = lax.axis_index("jobs"), lax.axis_index("tm")
    z, c = lax.div(mj, CORES), lax.rem(mj, CORES)
    x, y = lax.div(mt, ny), lax.rem(mt, ny)

    def zline(k):
        return lax.rem(z + k, RING) * CORES + c

    sibling = (z * CORES + 1 - c, mt)
    above, below = (zline(1), mt), (zline(RING - 1), mt)
    after, before = (mj, lax.rem(mt + 1, ntm)), (mj, lax.rem(mt + ntm - 1, ntm))
    z_peers = [(lax.rem(z + k, RING), (zline(k), mt)) for k in range(1, RING)]
    y_peers = [(lax.rem(y + k, ny), (mj, x * ny + lax.rem(y + k, ny))) for k in range(1, ny)]
    x_peers = [(lax.rem(x + k, nx), (mj, lax.rem(x + k, nx) * ny + y)) for k in range(1, nx)]

    t_peers = [(lax.rem(mt + k, ntm), (mj, lax.rem(mt + k, ntm))) for k in range(1, ntm)]
    tool, dur, rel, slack = (r.ints.at[k] for k in range(4))
    jw, assign = (r.floats.at[k] for k in range(2))

    sent = []

    def remote(src, dst, ssem, rsem, device):
        return pltpu.make_async_remote_copy(
            src_ref=src, dst_ref=dst, send_sem=ssem, recv_sem=rsem,
            device_id=device, device_id_type=pl.DeviceIdType.MESH,
        )

    def send(*args):
        copy = remote(*args)
        copy.start()
        sent.append(copy)

    def arrived(dst, ssem, rsem, device):
        remote(dst, dst, ssem, rsem, device).wait_recv()

    def drain():
        for copy in sent:
            copy.wait_send()
        sent.clear()

    def spread(buf, mine, peers, ssem, rsem):
        for k, (_, device) in enumerate(peers):
            send(buf.at[mine], buf.at[mine], ssem.at[k], rsem.at[mine], device)

        def wait():
            for k, (index, device) in enumerate(peers):
                arrived(buf.at[index], ssem.at[k], rsem.at[index], device)

        return wait

    def added(buf):
        total = buf[0]
        for k in range(1, buf.shape[0]):
            total = total + buf[k]
        return total

    barrier = pltpu.get_barrier_semaphore()
    partners = [sibling, above, below, before, after]
    partners += [device for group in (y_peers, x_peers) for _, device in group]
    for device in partners:
        pl.semaphore_signal(barrier, inc=1, device_id=device, device_id_type=pl.DeviceIdType.MESH)
    first_tool = pl.multiple_of(mj * share, share)
    loads = [
        pltpu.make_async_copy(source, target, r.s_load.at[k])
        for k, (source, target) in enumerate(
            [
                (tool_in, tool), (cap, r.cap_v), (sd, r.sd_v), (dur_in, dur), (rel_in, rel), (slack_in, slack),
                (jw_in, jw), (assign_in, assign), (eta_in, r.eta), (omega_in, r.omega),
                (capac.at[pl.ds(first_tool, share), :], r.capac_v),
            ]
        )
    ]
    for copy in loads:
        copy.start()
    loads[0].wait()

    lane = lax.broadcasted_iota(jnp.int32, (LANES, LANES), 1).astype(F32)

    @pl.loop(0, blocks)
    def _(b):
        row = jnp.broadcast_to(tool[pl.ds(b, 1), :].astype(F32), (LANES, LANES))
        column = row.T
        for k in range(tools // LANES):
            hit = jnp.where(column == lane + float(k * LANES), 1.0, 0.0).astype(BF16)
            r.mem[pl.ds(pl.multiple_of(b * LANES, LANES), LANES), k * LANES : (k + 1) * LANES] = hit

    loads[1].wait()

    @pl.loop(0, tools // share)
    def _(b):
        at = pl.ds(pl.multiple_of(b * share, share), share)
        high, low = split(r.cap_v[at, :])
        r.cap_hi[at, :] = high
        r.cap_lo[at, :] = low

    step = min(rows, 256)

    @pl.loop(0, rows // step)
    def _(b):
        at = pl.ds(pl.multiple_of(b * step, step), step)
        m = r.mem[at, :]
        found = dot(m, r.cap_hi[...]) + dot(m, r.cap_lo[...])
        r.pj0[WIN : WIN + slots, at] = found.T

    def lanes_of(b):
        return pl.ds(pl.multiple_of(b * LANES, LANES), LANES)

    slot = lax.broadcasted_iota(jnp.int32, (slots + WIN, LANES), 0) + (mt * slots - WIN)
    own = slice(WIN, WIN + slots)

    def allowed_of(b, s=slot):
        return (s >= rel[pl.ds(b, 1), :]) & (s + dur[pl.ds(b, 1), :] <= all_slots)

    def cost_of(b, s=slot):
        d = dur[pl.ds(b, 1), :]
        due = rel[pl.ds(b, 1), :] + d + slack[pl.ds(b, 1), :]
        end = s + d
        late = jnp.maximum(end - due, 0)
        return jw[pl.ds(b, 1), :] * (
            end.astype(F32) * (1.0 / all_slots) + late.astype(F32) * (1.0 / (4 * WIN))
        )

    for copy in loads[2:]:
        copy.wait()
    weight, eta = r.omega[0], r.eta[0]
    tau1, sigma1 = eta / weight, eta * weight

    @pl.loop(0, blocks)
    def _(b):
        start = r.sd_v[lanes_of(b), :].T
        p = jnp.where(allowed_of(b, slot[WIN:]), start, 0.0)
        r.p0[own, lanes_of(b)] = p
        r.yrow[y, pl.ds(blocks + b, 1), :] = fold(p)

    pl.semaphore_wait(barrier, len(partners))

    def halo(k, src, dst, device):
        send(src, dst, r.s_halo.at[0, k], r.s_halo.at[1, k], device)

    def halo_arrived(k, dst, device):
        arrived(dst, r.s_halo.at[0, k], r.s_halo.at[1, k], device)

    lead, head = pl.ds(0, WIN), pl.ds(WIN, WIN)
    tail, beyond = pl.ds(slots, WIN), pl.ds(slots + WIN, WIN)

    def exchange(k, buf):
        halo(k, buf.at[head, :], buf.at[beyond, :], before)
        halo(k + 1, buf.at[tail, :], buf.at[lead, :], after)

        def wait():
            halo_arrived(k, buf.at[beyond, :], after)
            halo_arrived(k + 1, buf.at[lead, :], before)

        return wait

    duals_wait = exchange(0, r.pj0)
    halo(2, r.p0.at[tail, :], r.p0.at[lead, :], after)

    r.cap_s[...] = r.cap_v[pl.ds(first_tool, share), :].T
    r.capac_s[...] = r.capac_v[...].astype(F32).T

    def adjoint(buf, b):
        at = lanes_of(b)
        past = jnp.where(mt == ntm - 1, 0.0, buf[beyond, at])
        x = jnp.concatenate([buf[0 : slots + WIN, at], past], axis=0)
        return window(x, dur[pl.ds(b, 1), :], False)[: slots + WIN] * (1.0 / WIN)

    def loaded(x, b):
        return window(x, dur[pl.ds(b, 1), :], True)[WIN:]

    def keep(w, b, first=0):
        high, low = split(w)
        n = w.shape[0]
        r.ws[first : first + n, lanes_of(b)] = high
        r.ws[slots + first : slots + first + n, lanes_of(b)] = low

    inner = slice(WIN, slots)
    r.accp[...] = jnp.zeros_like(r.accp)

    def updated(b, s, p, adj):
        gradient = cost_of(b, s) - assign[pl.ds(b, 1), :] * (1.0 / root) + adj * (1.0 / WIN)
        return jnp.where(allowed_of(b, s), jnp.maximum(p - tau1 * gradient, 0.0), 0.0)

    @pl.loop(0, blocks)
    def _(b):
        at = lanes_of(b)
        p = r.p0[inner, at]
        adj = window(r.pj0[own, at], dur[pl.ds(b, 1), :], False)[: slots - WIN]
        new = updated(b, slot[inner], p, adj)
        r.p1[inner, at] = new
        r.yrow[y, pl.ds(b, 1), :] = fold(new)
        moved = new - p
        r.accp[0:1, :] += fold(moved * moved)
        w = loaded(2.0 * new - p, b)
        r.wdp[WIN : slots - WIN, at] = 0.5 * (w - loaded(p, b))
        keep(w, b, WIN)

    duals_wait()
    halo_arrived(2, r.p0.at[lead, :], before)
    low, high = slice(0, WIN), slice(2 * WIN, 3 * WIN)
    edges = jnp.concatenate([slot[:WIN], slot[slots:]], axis=0)

    @pl.loop(0, blocks)
    def _(b):
        at = lanes_of(b)
        past = jnp.where(mt == ntm - 1, 0.0, r.pj0[beyond, at])
        bands = jnp.concatenate([r.pj0[: 2 * WIN, at], r.pj0[tail, at], past], axis=0)
        adj = window(bands, dur[pl.ds(b, 1), :], False)
        adj = jnp.concatenate([adj[low], adj[high]], axis=0)
        p = jnp.concatenate([r.p0[lead, at], r.p0[tail, at]], axis=0)
        p = jnp.where(allowed_of(b, edges), p, 0.0)
        new = updated(b, edges, p, adj)
        r.p1[lead, at] = new[:WIN]
        r.p1[tail, at] = new[WIN:]
        r.yrow[y, pl.ds(b, 1), :] += fold(new[WIN:])
        moved = (new - p)[WIN:]
        r.accp[0:1, :] += fold(moved * moved)
        inside = pl.ds(slots - WIN, WIN)
        old = jnp.concatenate([p[:WIN], r.p0[head, at], r.p0[inside, at], p[WIN:]], axis=0)
        now = jnp.concatenate([new[:WIN], r.p1[head, at], r.p1[inside, at], new[WIN:]], axis=0)
        w, v = (window(x, dur[pl.ds(b, 1), :], True) for x in (2.0 * now - old, old))
        for first, k in ((0, WIN), (slots - WIN, 3 * WIN)):
            r.wdp[first : first + WIN, at] = 0.5 * (w[k : k + WIN] - v[k : k + WIN])
            keep(w[k : k + WIN], b, first)

    rows_y = spread(r.yrow, y, y_peers, r.s_rowy.at[0, 0], r.s_rowy.at[0, 1])

    def rows_of(side, q):
        return pl.ds(side * half + q * piece, piece)

    def reduced_loads(it, extra, finish):
        paired = set()

        def produce(i):
            owner = lax.rem(z + ORDER[i], RING)
            full = dot(r.ws[...], r.mem[:, pl.ds(pl.multiple_of(owner * pair, pair), pair)])
            full = (full[:slots] + full[slots:]) * (1.0 / WIN)
            r.part[i, 0] = full[:, :share]
            r.part[i, 1] = full[:, share:]
            send(r.part.at[i, 1 - c], r.pairbuf.at[it, i], r.s_pair.at[it, 0, i], r.s_pair.at[it, 1, i], sibling)

        def mine(i, side, q):
            if i not in paired:
                arrived(r.pairbuf.at[it, i], r.s_pair.at[it, 0, i], r.s_pair.at[it, 1, i], sibling)
                paired.add(i)
            at = rows_of(side, q)
            return r.part[i, c, at, :] + r.pairbuf[it, i, at, :]

        def incoming(upward, m, q):
            buf, sems, source = (r.rsu, r.s_up, below) if upward else (r.rsd, r.s_dn, above)
            arrived(buf.at[it, m, q], sems.at[it, 0, m, q], sems.at[it, 1, m, q], source)
            return buf[it, m, q]

        def message(m, q, upward):
            buf, sems, to = (r.rsu, r.s_up, above) if upward else (r.rsd, r.s_dn, below)
            distance = 4 - (m + 1) // 2
            i = ORDER.index(distance if upward else RING - distance)
            side = m % 2 if upward else 1 - m % 2
            value = mine(i, side, q)
            if m >= 2:
                value = value + incoming(upward, m - 2, q)
            at = rows_of(side, q)
            r.part[i, c, at, :] = value
            send(r.part.at[i, c, at, :], buf.at[it, m, q], sems.at[it, 0, m, q], sems.at[it, 1, m, q], to)

        ready = {0: 3, 1: 3, 2: 5, 3: 5, 4: 7, 5: 7}
        done = 0
        for m in range(MESSAGES):
            while done < ready.get(m, RING):
                produce(done)
                done += 1
            for q in range(PIECES):
                message(m, q, True)
                message(m, q, False)
            extra(m)
        i = ORDER.index(0)
        for q in range(PIECES):
            for side in (0, 1):
                value = mine(i, side, q) + incoming(True, 6 - side, q) + incoming(False, 5 + side, q)
                finish(side, q, rows_of(side, q), value)

    def rows_first(m):
        if m == 3:
            rows_y()
            r.xrow[x] = added(r.yrow)
            rows_first.wait = spread(r.xrow, x, x_peers, r.s_rowx.at[0, 0], r.s_rowx.at[0, 1])
        if m == MESSAGES + 1:
            rows_first.wait()
            total = added(r.xrow)
            new, old = total[:blocks], total[blocks:]
            r.tot1[...] = new
            delta = sigma1 * (root - (2.0 * new - old) * (1.0 / root))
            r.a1[...] = assign[...] + delta
            once = jnp.where(mt == 0, 1.0, 0.0)
            r.accp[3:4, :] = once * fold(delta * delta)
            r.accp[4:5, :] = once * fold(delta * (new - old))

    def part_of(hops, side, q=None):
        at = pl.ds(side * half, half) if q is None else rows_of(side, q)
        return (lax.rem(z + hops + RING, RING), c, at, slice(None))

    def pass_on(m, q, upward):
        sems, to = (r.s_up, above) if upward else (r.s_dn, below)
        hops = -(m // 2) if upward else m // 2
        at = part_of(hops, m % 2 if upward else 1 - m % 2, q)
        send(r.ag.at[at], r.ag.at[at], sems.at[0, 2, m, q], sems.at[1, 2, m, q], to)

    def across(hops, side):
        k = 2 * (hops % RING) + side
        at = part_of(hops, side)
        send(r.ag.at[at], r.ag.at[at], r.s_sib.at[0, k], r.s_sib.at[1, k], sibling)

    def finish_first(side, q, at, value):
        old = r.cap_s[at, :]
        new = jnp.maximum(old + sigma1 * (value - r.capac_s[at, :]), 0.0)
        r.ag[z, c, at, :] = new
        pass_on(side, q, True)
        pass_on(1 - side, q, False)
        moved = new - old
        r.accp[1:2, :] += fold(moved * moved)
        if q == PIECES - 1:
            across(0, side)

    reduced_loads(0, rows_first, finish_first)

    def crossed(hops, side):
        k = 2 * (hops % RING) + side
        at = (lax.rem(z + hops + RING, RING), 1 - c, pl.ds(side * half, half), slice(None))
        arrived(r.ag.at[at], r.s_sib.at[0, k], r.s_sib.at[1, k], sibling)

    def gather(hops, first=False):
        crossed(hops, 0)
        crossed(hops, 1)
        owner = lax.rem(z + hops + RING, RING)
        high, low = split(jnp.concatenate([r.ag[owner, 0], r.ag[owner, 1]], axis=1))
        both = jnp.concatenate([high, low], axis=0)
        full = dot(both, r.mem[:, pl.ds(pl.multiple_of(owner * pair, pair), pair)], 1)
        full = full[:slots] + full[slots:]
        r.pj1[own, :] = full if first else r.pj1[own, :] + full

    work = {1: (0,), 3: (-1, 1), 5: (-2, 2), 6: (-3, 3)}
    for m in range(MESSAGES):
        for upward in (True, False):
            hops = -1 - m // 2 if upward else 1 + m // 2
            side = m % 2 if upward else 1 - m % 2
            sems, source = (r.s_up, below) if upward else (r.s_dn, above)
            for q in range(PIECES):
                arrived(r.ag.at[part_of(hops, side, q)], sems.at[0, 2, m, q], sems.at[1, 2, m, q], source)
                if m + 2 < MESSAGES:
                    pass_on(m + 2, q, upward)
            across(hops, side)
        for hops in work.get(m, ()):
            gather(hops, first=hops == 0)
        rows_first(MESSAGES + m)
    gather(4)

    duals_wait = exchange(3, r.pj1)

    @pl.loop(0, blocks)
    def _(b):
        at = lanes_of(b)
        r.accp[2:3, :] += fold((r.pj1[own, at] - r.pj0[own, at]) * r.wdp[:, at]) * (1.0 / WIN)

    r.sc_c[c] = r.accp[...]
    spread(r.sc_c, c, [(1 - c, sibling)], r.s_scc.at[0], r.s_scc.at[1])()
    r.sc_z[z] = added(r.sc_c)
    sums_wait = spread(r.sc_z, z, z_peers, r.s_scz.at[0], r.s_scz.at[1])
    sums_wait()
    r.sc_t[mt] = added(r.sc_z)
    sums_wait = spread(r.sc_t, mt, t_peers, r.s_sct.at[0], r.s_sct.at[1])
    duals_wait()

    @pl.loop(0, blocks)
    def _(b):
        r.grad[:, lanes_of(b)] = cost_of(b) - r.a1[pl.ds(b, 1), :] * (1.0 / root) + adjoint(r.pj1, b)

    sums_wait()
    sums = jnp.sum(added(r.sc_t), axis=1, keepdims=True)
    sum_primal, sum_cap, cross_primal, sum_assign, cross_assign = (sums[k : k + 1] for k in range(5))
    movement = weight * 0.5 * sum_primal + (sum_assign + sum_cap) / (2.0 * weight)
    interaction = jnp.abs(cross_primal - cross_assign * (1.0 / root))
    step_next = movement / (interaction + movement / (1.5 * eta))
    tau2 = jnp.broadcast_to(step_next / weight, (1, LANES))
    sigma2 = jnp.broadcast_to(step_next * weight, (1, LANES))

    drain()

    @pl.loop(0, blocks)
    def _(b):
        at = lanes_of(b)
        p = r.p1[:, at]
        new = jnp.where(allowed_of(b), jnp.maximum(p - tau2 * r.grad[:, at], 0.0), 0.0)
        r.p0[:, at] = new
        r.yrow2[y, pl.ds(b, 1), :] = fold(new[WIN:])
        keep(loaded(2.0 * new - p, b), b)

    rows2_y = spread(r.yrow2, y, y_peers, r.s_rowy.at[1, 0], r.s_rowy.at[1, 1])

    store = pltpu.make_async_copy(r.sd_v, out_p, r.s_out.at[0])

    def rows_second(m):
        if m == 3:
            rows2_y()
            r.xrow2[x] = added(r.yrow2)
            rows_second.wait = spread(r.xrow2, x, x_peers, r.s_rowx.at[1, 0], r.s_rowx.at[1, 1])
        if m == 5:
            rows_second.wait()
            new = added(r.xrow2)
            out_a[...] = r.a1[...] + sigma2 * (root - (2.0 * new - r.tot1[...]) * (1.0 / root))

        if m == 3:

            @pl.loop(0, blocks)
            def _(b):
                r.sd_v[lanes_of(b), :] = r.p0[own, lanes_of(b)].T

            store.start()

    def finish_second(side, q, at, value):
        r.c2[at, :] = jnp.maximum(r.ag[z, c, at, :] + sigma2 * (value - r.capac_s[at, :]), 0.0)

    reduced_loads(1, rows_second, finish_second)
    out_c[...] = r.c2[...].T
    drain()
    store.wait()


def move(*refs):
    n = len(refs) // 2
    sems = refs[-1]
    copies = [pltpu.make_async_copy(refs[k], refs[n + k], sems.at[k]) for k in range(n)]
    for copy in copies:
        copy.start()
    for copy in copies:
        copy.wait()


def shards(sizes, all_slots, start, assign, cap, tool, dur, rel, slack, capac, jw, eta, omega):
    ny, nx = sizes
    rows, slots = start.shape
    tools = cap.shape[0]
    share = tools // (RING * CORES)
    blocks = rows // LANES
    scratch = scratch_of(rows, slots, tools, share, blocks, ny, nx)
    hbm = pl.BlockSpec(memory_space=pltpu.HBM)
    vec = pl.BlockSpec(memory_space=pltpu.VMEM)

    def tiles(v):
        return v.reshape(blocks, LANES)

    results = (
        jax.ShapeDtypeStruct((rows, slots), F32),
        jax.ShapeDtypeStruct((blocks, LANES), F32),
        jax.ShapeDtypeStruct((share, slots), F32),
    )
    found = pl.pallas_call(
        functools.partial(kernel, tuple(scratch), ny, nx, all_slots),
        out_shape=results,
        in_specs=[hbm] * 11,
        out_specs=(hbm, vec, vec),
        scratch_shapes=list(scratch.values()),
        compiler_params=pltpu.CompilerParams(
            collective_id=0, has_side_effects=True, vmem_limit_bytes=58 * 1024 * 1024
        ),
        cost_estimate=pl.CostEstimate(flops=8_600_000_000, bytes_accessed=6_000_000, transcendentals=0),
        name="pdhg",
    )(start, cap, capac, *map(tiles, (tool, dur, rel, slack, jw, assign)), eta, omega)
    p, a, c = pl.pallas_call(
        move,
        out_shape=results,
        in_specs=[vec] * 3,
        out_specs=(hbm, hbm, hbm),
        scratch_shapes=[pltpu.SemaphoreType.DMA((3,))],
        name="move",
    )(*found)
    return p, a.reshape(rows), c


def solution(mesh):
    ntm = mesh.shape["tm"]
    ny = 4 if ntm >= 16 else ntm

    def run(start, *rest):
        body = functools.partial(shards, (ny, ntm // ny), start.shape[1])
        return jax.shard_map(
            body,
            mesh=mesh,
            in_specs=(
                P("jobs", "tm"), P("jobs"), P(None, "tm"), P("jobs"), P("jobs"), P("jobs"),
                P("jobs"), P(None, "tm"), P("jobs"), P(), P(),
            ),
            out_specs=(P("jobs", "tm"), P("jobs"), P("jobs", "tm")),
            check_vma=False,
        )(start, *rest)

    return run
```

time: 104 us -> 92.6 us (0.89)
  Pallas kernels: 97.9 us -> 90.6 us
  local copies, waits for them, and re-layouts: 3.55 us -> 0 us
    pallas_call x1, Pallas kernels: 97.9 us -> 88.3 us  [shards(): pl.pallas_call(functools.partial(kernel, tuple(scratch), ny, nx, all_slot...]
    unnamed x7 -> x0, local copies, waits for them, and re-layouts: 3.55 us -> none
    pallas_call x0 -> x1, Pallas kernels: none -> 2.26 us  [shards(): pl.pallas_call(move, out_shape=results, in_specs=[vec] * 3, out_specs=(hb...]
where the time goes in v2:
time: 92.6 us; the launch traced here: 92.5 us
  Pallas kernels  90.6 us (98%)
  between operations  1.93 us (2%)
    pallas_call x1, Pallas kernels, shards(): pl.pallas_call(functools.partial(kernel, tuple(scratch), ny, nx, all_slot...  88.3 us
    pallas_call x1, Pallas kernels, shards(): pl.pallas_call(move, out_shape=results, in_specs=[vec] * 3, out_specs=(hb...  2.26 us

profile of v2, /device:TPU:8, one launch (start us, length us, event | category | flops | bytes accessed | tf_op | source)
XLA Modules:
  0.0 92.5 jit_solution(5089633146806593567)
XLA Ops:
  1.9 88.3 %pdhg.1 = (f32[1024,256]{1,0:T(8,128)}, f32[8,128]{1,0:T(8,128)}, f32[128,256]{1,0:T(8,128)}) custom-call(f32[1024,256]{1,0:T(8,128)} %sd.1, f32[2048,256]{1,0:T(8,128)} %cap.1, s32[2048,256]{1,0:T(8,128)} %capac.1, s32[8,128]{1,0:T(8,128)} %bitcast.7, s32[8,128]{1,0:T(8,128)} %bitcast.8, s32[8,128]{1,0:T(8,128)} %bitcast.9, s32[8,128]{1,0:T(8,128)} %bitcast.10, ...), custom_call_target="tpu_custom_call" | custom-call | flops 8600000512 | bytes 6000000 | tf_op jit(solution)/shard_map/pdhg/pallas_call | solution.py:574
  90.2 2.3 %move.1 = (f32[1024,256]{1,0:T(8,128)}, f32[8,128]{1,0:T(8,128)}, f32[128,256]{1,0:T(8,128)}) custom-call(f32[1024,256]{1,0:T(8,128)} %get-tuple-element.9.refs_0_, f32[8,128]{1,0:T(8,128)} %get-tuple-element.10.refs_1_, f32[128,256]{1,0:T(8,128)} %get-tuple-element.11.refs_2_), custom_call_target="tpu_custom_call" | custom-call | tf_op jit(solution)/shard_map/move/pallas_call | solution.py:586

commit v3 on v2

--- a/solution.py
+++ b/solution.py
@@ -17,6 +17,7 @@
 ORDER = (4, 3, 5, 2, 6, 1, 7, 0)
 MESSAGES = 7
 PIECES = 2
+STRIPS = 4
 
 
 def window(x, dur, backward):
@@ -34,6 +35,13 @@
         acc = jnp.where((d & span) != 0, total + move(acc, span), acc)
     total = total + move(total, span)
     return jnp.where(d == WIN, total, acc)
+
+
+def summed(x, dur, backward):
+    half = (x.shape[0] - WIN) // 2
+    parts = (x[: half + WIN], x[half:])
+    kept = slice(WIN, None) if backward else slice(0, half)
+    return jnp.concatenate([window(part, dur, backward)[kept] for part in parts], axis=0)
 
 
 def split(x):
@@ -87,8 +95,7 @@
         tot1=vmem((blocks, LANES), F32),
         a1=vmem((blocks, LANES), F32),
         accp=vmem((8, LANES), F32),
-        sc_c=vmem((CORES, 8, LANES), F32),
-        sc_z=vmem((RING, 8, LANES), F32),
+        sc_j=vmem((RING * CORES, 8, LANES), F32),
         sc_t=vmem((ny * nx, 8, LANES), F32),
         s_load=dma((11,)),
         s_out=dma((1,)),
@@ -99,8 +106,7 @@
         s_sib=dma((2, 2 * RING)),
         s_rowy=dma((2, 2, ny)),
         s_rowx=dma((2, 2, nx)),
-        s_scc=dma((2, CORES)),
-        s_scz=dma((2, RING)),
+        s_scj=dma((2, RING * CORES)),
         s_sct=dma((2, ny * nx)),
     )
 
@@ -127,7 +133,8 @@
     sibling = (z * CORES + 1 - c, mt)
     above, below = (zline(1), mt), (zline(RING - 1), mt)
     after, before = (mj, lax.rem(mt + 1, ntm)), (mj, lax.rem(mt + ntm - 1, ntm))
-    z_peers = [(lax.rem(z + k, RING), (zline(k), mt)) for k in range(1, RING)]
+    far = sorted(range(1, RING * CORES), key=lambda k: -min(k, RING * CORES - k))
+    j_peers = [(lax.rem(mj + k, RING * CORES), (lax.rem(mj + k, RING * CORES), mt)) for k in far]
     y_peers = [(lax.rem(y + k, ny), (mj, x * ny + lax.rem(y + k, ny))) for k in range(1, ny)]
     x_peers = [(lax.rem(x + k, nx), (mj, lax.rem(x + k, nx) * ny + y)) for k in range(1, nx)]
 
@@ -281,10 +288,10 @@
         at = lanes_of(b)
         past = jnp.where(mt == ntm - 1, 0.0, buf[beyond, at])
         x = jnp.concatenate([buf[0 : slots + WIN, at], past], axis=0)
-        return window(x, dur[pl.ds(b, 1), :], False)[: slots + WIN] * (1.0 / WIN)
+        return summed(x, dur[pl.ds(b, 1), :], False) * (1.0 / WIN)
 
     def loaded(x, b):
-        return window(x, dur[pl.ds(b, 1), :], True)[WIN:]
+        return summed(x, dur[pl.ds(b, 1), :], True)
 
     def keep(w, b, first=0):
         high, low = split(w)
@@ -303,7 +310,7 @@
     def _(b):
         at = lanes_of(b)
         p = r.p0[inner, at]
-        adj = window(r.pj0[own, at], dur[pl.ds(b, 1), :], False)[: slots - WIN]
+        adj = summed(r.pj0[own, at], dur[pl.ds(b, 1), :], False)
         new = updated(b, slot[inner], p, adj)
         r.p1[inner, at] = new
         r.yrow[y, pl.ds(b, 1), :] = fold(new)
@@ -479,12 +486,9 @@
         at = lanes_of(b)
         r.accp[2:3, :] += fold((r.pj1[own, at] - r.pj0[own, at]) * r.wdp[:, at]) * (1.0 / WIN)
 
-    r.sc_c[c] = r.accp[...]
-    spread(r.sc_c, c, [(1 - c, sibling)], r.s_scc.at[0], r.s_scc.at[1])()
-    r.sc_z[z] = added(r.sc_c)
-    sums_wait = spread(r.sc_z, z, z_peers, r.s_scz.at[0], r.s_scz.at[1])
-    sums_wait()
-    r.sc_t[mt] = added(r.sc_z)
+    r.sc_j[mj] = r.accp[...]
+    spread(r.sc_j, mj, j_peers, r.s_scj.at[0], r.s_scj.at[1])()
+    r.sc_t[mt] = added(r.sc_j)
     sums_wait = spread(r.sc_t, mt, t_peers, r.s_sct.at[0], r.s_sct.at[1])
     duals_wait()
 
@@ -543,13 +547,20 @@
     store.wait()
 
 
-def move(*refs):
-    n = len(refs) // 2
-    sems = refs[-1]
-    copies = [pltpu.make_async_copy(refs[k], refs[n + k], sems.at[k]) for k in range(n)]
-    for copy in copies:
+def move(p, a, c, p_out, a_out, c_out, p_v, a_v, c_v, sem_in, sem_out):
+    rows = p.shape[0] // STRIPS
+    ways = [(a, a_v, a_out), (c, c_v, c_out)]
+    for k in range(STRIPS):
+        at = pl.ds(k * rows, rows)
+        ways.append((p.at[at, :], p_v.at[at, :], p_out.at[at, :]))
+    copies_in = [pltpu.make_async_copy(w[0], w[1], sem_in.at[k]) for k, w in enumerate(ways)]
+    copies_out = [pltpu.make_async_copy(w[1], w[2], sem_out.at[k]) for k, w in enumerate(ways)]
+    for copy in copies_in:
         copy.start()
-    for copy in copies:
+    for before, after in zip(copies_in, copies_out):
+        before.wait()
+        after.start()
+    for copy in copies_out:
         copy.wait()
 
 
@@ -586,9 +597,10 @@
     p, a, c = pl.pallas_call(
         move,
         out_shape=results,
-        in_specs=[vec] * 3,
+        in_specs=[hbm] * 3,
         out_specs=(hbm, hbm, hbm),
-        scratch_shapes=[pltpu.SemaphoreType.DMA((3,))],
+        scratch_shapes=[pltpu.VMEM(result.shape, F32) for result in results]
+        + [pltpu.SemaphoreType.DMA((2 + STRIPS,))] * 2,
         name="move",
     )(*found)
     return p, a.reshape(rows), c

time: 92.6 us -> 91.2 us (0.985)
  Pallas kernels: 90.6 us -> 89 us
    pallas_call x1, Pallas kernels: 88.3 us -> 87 us  [shards(): pl.pallas_call(functools.partial(kernel, tuple(scratch), ny, nx, all_slot...]
where the time goes in v3:
time: 91.2 us; the launch traced here: 91 us
  Pallas kernels  89 us (98%)
  between operations  1.93 us (2%)
    pallas_call x1, Pallas kernels, shards(): pl.pallas_call(functools.partial(kernel, tuple(scratch), ny, nx, all_slot...  87 us
    pallas_call x1, Pallas kernels, shards(): pl.pallas_call(move, out_shape=results, in_specs=[hbm] * 3, out_specs=(hb...  2.09 us

profile of v3, /device:TPU:8, one launch (start us, length us, event | category | flops | bytes accessed | tf_op | source)
XLA Modules:
  0.0 91.0 jit_solution(12051807969234085654)
XLA Ops:
  1.9 87.0 %pdhg.1 = (f32[1024,256]{1,0:T(8,128)}, f32[8,128]{1,0:T(8,128)}, f32[128,256]{1,0:T(8,128)}) custom-call(f32[1024,256]{1,0:T(8,128)} %sd.1, f32[2048,256]{1,0:T(8,128)} %cap.1, s32[2048,256]{1,0:T(8,128)} %capac.1, s32[8,128]{1,0:T(8,128)} %bitcast.7, s32[8,128]{1,0:T(8,128)} %bitcast.8, s32[8,128]{1,0:T(8,128)} %bitcast.9, s32[8,128]{1,0:T(8,128)} %bitcast.10, ...), custom_call_target="tpu_custom_call" | custom-call | flops 8600000512 | bytes 6000000 | tf_op jit(solution)/shard_map/pdhg/pallas_call | solution.py:585
  88.9 2.1 %move.1 = (f32[1024,256]{1,0:T(8,128)}, f32[8,128]{1,0:T(8,128)}, f32[128,256]{1,0:T(8,128)}) custom-call(f32[1024,256]{1,0:T(8,128)} %get-tuple-element.9.p, f32[8,128]{1,0:T(8,128)} %get-tuple-element.10.a, f32[128,256]{1,0:T(8,128)} %get-tuple-element.11.c), custom_call_target="tpu_custom_call" | custom-call | tf_op jit(solution)/shard_map/move/pallas_call | solution.py:597

commit v4 on v3

--- a/solution.py
+++ b/solution.py
@@ -138,7 +138,10 @@
     y_peers = [(lax.rem(y + k, ny), (mj, x * ny + lax.rem(y + k, ny))) for k in range(1, ny)]
     x_peers = [(lax.rem(x + k, nx), (mj, lax.rem(x + k, nx) * ny + y)) for k in range(1, nx)]
 
-    t_peers = [(lax.rem(mt + k, ntm), (mj, lax.rem(mt + k, ntm))) for k in range(1, ntm)]
+    moves = [(i, j) for i in range(nx) for j in range(ny) if i or j]
+    moves.sort(key=lambda v: -min(v[0], nx - v[0]) - min(v[1], ny - v[1]))
+    t_peers = [lax.rem(x + i, nx) * ny + lax.rem(y + j, ny) for i, j in moves]
+    t_peers = [(k, (mj, k)) for k in t_peers]
     tool, dur, rel, slack = (r.ints.at[k] for k in range(4))
     jw, assign = (r.floats.at[k] for k in range(2))
 
@@ -201,7 +204,7 @@
 
     lane = lax.broadcasted_iota(jnp.int32, (LANES, LANES), 1).astype(F32)
 
-    @pl.loop(0, blocks)
+    @pl.loop(0, blocks, unroll=2)
     def _(b):
         row = jnp.broadcast_to(tool[pl.ds(b, 1), :].astype(F32), (LANES, LANES))
         column = row.T
@@ -250,7 +253,7 @@
     weight, eta = r.omega[0], r.eta[0]
     tau1, sigma1 = eta / weight, eta * weight
 
-    @pl.loop(0, blocks)
+    @pl.loop(0, blocks, unroll=2)
     def _(b):
         start = r.sd_v[lanes_of(b), :].T
         p = jnp.where(allowed_of(b, slot[WIN:]), start, 0.0)
@@ -306,7 +309,7 @@
         gradient = cost_of(b, s) - assign[pl.ds(b, 1), :] * (1.0 / root) + adj * (1.0 / WIN)
         return jnp.where(allowed_of(b, s), jnp.maximum(p - tau1 * gradient, 0.0), 0.0)
 
-    @pl.loop(0, blocks)
+    @pl.loop(0, blocks, unroll=2)
     def _(b):
         at = lanes_of(b)
         p = r.p0[inner, at]
@@ -325,7 +328,7 @@
     low, high = slice(0, WIN), slice(2 * WIN, 3 * WIN)
     edges = jnp.concatenate([slot[:WIN], slot[slots:]], axis=0)
 
-    @pl.loop(0, blocks)
+    @pl.loop(0, blocks, unroll=2)
     def _(b):
         at = lanes_of(b)
         past = jnp.where(mt == ntm - 1, 0.0, r.pj0[beyond, at])
@@ -481,7 +484,7 @@
 
     duals_wait = exchange(3, r.pj1)
 
-    @pl.loop(0, blocks)
+    @pl.loop(0, blocks, unroll=2)
     def _(b):
         at = lanes_of(b)
         r.accp[2:3, :] += fold((r.pj1[own, at] - r.pj0[own, at]) * r.wdp[:, at]) * (1.0 / WIN)
@@ -492,7 +495,7 @@
     sums_wait = spread(r.sc_t, mt, t_peers, r.s_sct.at[0], r.s_sct.at[1])
     duals_wait()
 
-    @pl.loop(0, blocks)
+    @pl.loop(0, blocks, unroll=2)
     def _(b):
         r.grad[:, lanes_of(b)] = cost_of(b) - r.a1[pl.ds(b, 1), :] * (1.0 / root) + adjoint(r.pj1, b)
 
@@ -507,7 +510,7 @@
 
     drain()
 
-    @pl.loop(0, blocks)
+    @pl.loop(0, blocks, unroll=2)
     def _(b):
         at = lanes_of(b)
         p = r.p1[:, at]
@@ -532,7 +535,7 @@
 
         if m == 3:
 
-            @pl.loop(0, blocks)
+            @pl.loop(0, blocks, unroll=2)
             def _(b):
                 r.sd_v[lanes_of(b), :] = r.p0[own, lanes_of(b)].T
 

time: 91.2 us -> 90.6 us (level)
  no operation moved by 1% of the time
where the time goes in v4:
time: 90.6 us; the launch traced here: 90.4 us
  Pallas kernels  88.5 us (98%)
  between operations  1.93 us (2%)
    pallas_call x1, Pallas kernels, shards(): pl.pallas_call(functools.partial(kernel, tuple(scratch), ny, nx, all_slot...  86.4 us
    pallas_call x1, Pallas kernels, shards(): pl.pallas_call(move, out_shape=results, in_specs=[hbm] * 3, out_specs=(hb...  2.09 us

profile of v4, /device:TPU:8, one launch (start us, length us, event | category | flops | bytes accessed | tf_op | source)
XLA Modules:
  0.0 90.4 jit_solution(12264754073726775441)
XLA Ops:
  1.9 86.4 %pdhg.1 = (f32[1024,256]{1,0:T(8,128)}, f32[8,128]{1,0:T(8,128)}, f32[128,256]{1,0:T(8,128)}) custom-call(f32[1024,256]{1,0:T(8,128)} %sd.1, f32[2048,256]{1,0:T(8,128)} %cap.1, s32[2048,256]{1,0:T(8,128)} %capac.1, s32[8,128]{1,0:T(8,128)} %bitcast.7, s32[8,128]{1,0:T(8,128)} %bitcast.8, s32[8,128]{1,0:T(8,128)} %bitcast.9, s32[8,128]{1,0:T(8,128)} %bitcast.10, ...), custom_call_target="tpu_custom_call" | custom-call | flops 8600000512 | bytes 6000000 | tf_op jit(solution)/shard_map/pdhg/pallas_call | solution.py:588
  88.3 2.1 %move.1 = (f32[1024,256]{1,0:T(8,128)}, f32[8,128]{1,0:T(8,128)}, f32[128,256]{1,0:T(8,128)}) custom-call(f32[1024,256]{1,0:T(8,128)} %get-tuple-element.9.p, f32[8,128]{1,0:T(8,128)} %get-tuple-element.10.a, f32[128,256]{1,0:T(8,128)} %get-tuple-element.11.c), custom_call_target="tpu_custom_call" | custom-call | tf_op jit(solution)/shard_map/move/pallas_call | solution.py:600

commit v5 on v4

--- a/solution.py
+++ b/solution.py
@@ -391,7 +391,7 @@
             r.part[i, c, at, :] = value
             send(r.part.at[i, c, at, :], buf.at[it, m, q], sems.at[it, 0, m, q], sems.at[it, 1, m, q], to)
 
-        ready = {0: 3, 1: 3, 2: 5, 3: 5, 4: 7, 5: 7}
+        ready = {0: 2, 1: 3, 2: 5, 3: 5, 4: 7, 5: 7}
         done = 0
         for m in range(MESSAGES):
             while done < ready.get(m, RING):

time: 90.6 us -> 90.7 us (level)
  no operation moved by 1% of the time
where the time goes in v5:
time: 90.7 us; the launch traced here: 90.5 us
  Pallas kernels  88.6 us (98%)
  between operations  1.93 us (2%)
    pallas_call x1, Pallas kernels, shards(): pl.pallas_call(functools.partial(kernel, tuple(scratch), ny, nx, all_slot...  86.5 us
    pallas_call x1, Pallas kernels, shards(): pl.pallas_call(move, out_shape=results, in_specs=[hbm] * 3, out_specs=(hb...  2.09 us

profile of v5, /device:TPU:8, one launch (start us, length us, event | category | flops | bytes accessed | tf_op | source)
XLA Modules:
  0.0 90.5 jit_solution(8521109308218189522)
XLA Ops:
  1.9 86.5 %pdhg.1 = (f32[1024,256]{1,0:T(8,128)}, f32[8,128]{1,0:T(8,128)}, f32[128,256]{1,0:T(8,128)}) custom-call(f32[1024,256]{1,0:T(8,128)} %sd.1, f32[2048,256]{1,0:T(8,128)} %cap.1, s32[2048,256]{1,0:T(8,128)} %capac.1, s32[8,128]{1,0:T(8,128)} %bitcast.7, s32[8,128]{1,0:T(8,128)} %bitcast.8, s32[8,128]{1,0:T(8,128)} %bitcast.9, s32[8,128]{1,0:T(8,128)} %bitcast.10, ...), custom_call_target="tpu_custom_call" | custom-call | flops 8600000512 | bytes 6000000 | tf_op jit(solution)/shard_map/pdhg/pallas_call | solution.py:588
  88.4 2.1 %move.1 = (f32[1024,256]{1,0:T(8,128)}, f32[8,128]{1,0:T(8,128)}, f32[128,256]{1,0:T(8,128)}) custom-call(f32[1024,256]{1,0:T(8,128)} %get-tuple-element.9.p, f32[8,128]{1,0:T(8,128)} %get-tuple-element.10.a, f32[128,256]{1,0:T(8,128)} %get-tuple-element.11.c), custom_call_target="tpu_custom_call" | custom-call | tf_op jit(solution)/shard_map/move/pallas_call | solution.py:600
